TPU v7x, 512 devices: a whole 4x8x8 slice. The times are simulated.
512 devices in a mesh: dp: 32 (over x, y), list: 16 (over z, core).
Axes of the slice: x: 4, y: 8, z: 8, core: 2. Of those that a mesh axis runs over, the one named last changes fastest.
Arguments:
- points: bfloat16 [1048576, 1024], P(('dp', 'list')), may hold values from -16 to 16
- block_cluster: int32 [4096], P(('dp', 'list')), may hold values from 0 to 15, as said below
- block_rows: int32 [4096], P(('dp', 'list')), may hold values from 1 to 256, as said below
- coarse: bfloat16 [16, 1024], replicated, may hold values from -16 to 16
- fine: bfloat16 [16, 256, 1024], P('list'), may hold values from -16 to 16
Outputs:
- new_fine: float32 [16, 256, 1024], P('list', 'dp')
- coarse_shift: float32 [16, 1024], P('list')
Inputs may be any that keep to these rules, and one draw needn't show every extreme that they name: Within each device's 8 blocks the clusters rise, and no two of them have the same owner block_cluster. `block_rows`: the valid rows of a block come first.
All inputs are finite; a program needn't handle non-finite values.
Results may differ from a plain program's by a relative error of at most 0.006.
Values may be sent and summed in bfloat16 or wider, within the bound.
A program may use at most 128 MiB of HBM per device.

v0:
```python
import jax
import jax.numpy as jnp
from jax import lax
from jax.sharding import PartitionSpec as P


def per_device(points, block_cluster, block_rows, coarse, fine):
    owners = lax.axis_size("list")
    position = lax.axis_index("list")
    blocks = block_cluster.shape[0]
    per_owner = fine.shape[0]
    fine_count = fine.shape[1]
    coordinate_count = fine.shape[2]
    clusters = coarse.shape[0]
    block_len = points.shape[0] // blocks
    smoothing_divisor = coordinate_count / 32.0
    point_rows = points.reshape(blocks, block_len, coordinate_count)
    member = block_cluster[:, None] == jnp.arange(clusters, dtype=jnp.int32)[None, :]
    centre = jnp.dot(member.astype(jnp.bfloat16), coarse, preferred_element_type=jnp.float32)
    leftover_offsets = (point_rows.astype(jnp.float32) - centre[:, None, :]).astype(jnp.bfloat16)
    routing = (block_cluster // per_owner)[None, :] == jnp.arange(owners, dtype=jnp.int32)[:, None]
    outgoing = jnp.einsum(
        "ob,bnd->ond",
        routing.astype(jnp.bfloat16),
        leftover_offsets,
        preferred_element_type=jnp.bfloat16,
    )
    out_cluster = jnp.sum(jnp.where(routing, block_cluster[None, :], 0), axis=1)
    out_rows = jnp.sum(jnp.where(routing, block_rows[None, :], 0), axis=1)
    row_index = jnp.arange(block_len, dtype=jnp.int32)
    arrived, in_cluster, in_rows = (
        lax.all_to_all(outgoing, "list", split_axis=0, concat_axis=0, tiled=True),
        lax.all_to_all(out_cluster, "list", split_axis=0, concat_axis=0, tiled=True),
        lax.all_to_all(out_rows, "list", split_axis=0, concat_axis=0, tiled=True),
    )
    local_slot = jnp.clip(in_cluster - position * per_owner, 0, per_owner - 1)
    fine_norm = jnp.sum(jnp.square(fine.astype(jnp.float32)), axis=2)

    def absorb(carry, item):
        fine_sums, counts, drift_part, seen_part = carry
        resid_slot, cluster_slot, valid_rows = item
        group_centroid_matrix = lax.dynamic_index_in_dim(fine, cluster_slot, 0, keepdims=False)
        point_magnitudes = lax.dynamic_index_in_dim(fine_norm, cluster_slot, 0, keepdims=False)
        unscaled_scores = jnp.einsum(
            "nd,kd->nk", resid_slot, group_centroid_matrix, preferred_element_type=jnp.float32
        )
        membership_logits = (2.0 * unscaled_scores - point_magnitudes[None, :]) / smoothing_divisor
        live_mask = row_index < valid_rows
        highest = jnp.max(membership_logits, axis=1, keepdims=True)
        expo = jnp.exp(membership_logits - highest)
        weights = expo / jnp.sum(expo, axis=1, keepdims=True)
        weights = jnp.where(live_mask[:, None], weights, 0.0)
        weight_half = weights.astype(jnp.bfloat16)
        partial_value = jnp.einsum(
            "nk,nd->kd", weight_half, resid_slot, preferred_element_type=jnp.float32
        )
        fine_sums = fine_sums.at[cluster_slot].add(partial_value)
        counts = counts.at[cluster_slot].add(jnp.sum(weights, axis=0))
        kept_sum = jnp.sum(
            jnp.where(live_mask[:, None], resid_slot.astype(jnp.float32), 0.0), axis=0
        )
        drift_part = drift_part.at[cluster_slot].add(kept_sum)
        seen_part = seen_part.at[cluster_slot].add(valid_rows.astype(jnp.float32))
        return (fine_sums, counts, drift_part, seen_part)

    def visit(carry, item):
        return (absorb(carry, item), None)

    start = (
        jnp.zeros((per_owner, fine_count, coordinate_count), jnp.float32),
        jnp.zeros((per_owner, fine_count), jnp.float32),
        jnp.zeros((per_owner, coordinate_count), jnp.float32),
        jnp.zeros((per_owner,), jnp.float32),
    )
    carry, _ = lax.scan(visit, start, (arrived, local_slot, in_rows))
    fine_sums, counts, drift_part, seen_part = carry
    drift_sum, seen_rows = lax.psum((drift_part, seen_part), "dp")
    fine_sums, counts = (
        lax.psum_scatter(fine_sums, "dp", scatter_dimension=1, tiled=True),
        lax.psum_scatter(counts, "dp", scatter_dimension=1, tiled=True),
    )
    share_rows = fine_sums.shape[1]
    previous = lax.dynamic_slice_in_dim(
        fine, lax.axis_index("dp") * share_rows, share_rows, 1
    ).astype(jnp.float32)
    new_fine = (fine_sums + previous) / (counts[:, :, None] + 1.0)
    coarse_shift = drift_sum / (seen_rows[:, None] + 1.0)
    return (new_fine, coarse_shift)


def solution(mesh):
    placed = (
        P(("dp", "list"), None),
        P(("dp", "list")),
        P(("dp", "list")),
        P(),
        P("list", None, None),
    )
    return jax.shard_map(
        per_device,
        mesh=mesh,
        in_specs=placed,
        out_specs=(P("list", "dp", None), P("list", None)),
        check_vma=False,
    )
```

profile of v0, /device:TPU:16, one launch (start us, length us, event | category | flops | bytes accessed | tf_op | source)
XLA Modules:
  0.0 668.4 jit_solution(17947501884105106308)
XLA Ops:
  8.7 10.4 %all-to-all-start = ((s32[16,1,1]{2,1,0:T(1,128)}), s32[16,1,1]{2,1,0:T(1,128)S(1)}, u32[]{:S(2)}, u32[]{:S(2)}) async-start(s32[16,1,1]{2,1,0:T(1,128)} %copy.13), calls=%async_computation | async-start | bytes 16384 | tf_op jit(solution)/shard_map/all_to_all | solution.py:33
  20.6 6.5 convert.1
  27.1 7.2 %all-to-all-start.1 = ((s32[16,1,1]{2,1,0:T(1,128)}), s32[16,1,1]{2,1,0:T(1,128)S(1)}, u32[]{:S(2)}, u32[]{:S(2)}) async-start(s32[16,1,1]{2,1,0:T(1,128)} %copy.14), calls=%async_computation.1 | async-start | bytes 16384 | tf_op jit(solution)/shard_map/all_to_all | solution.py:34
  34.3 11.2 %fusion.16 = bf16[16,256,1024]{2,0,1:T(8,128)(2,1)} fusion(f32[8,256,1024]{2,1,0:T(8,128)} %convert.1, f32[8,1024]{1,0:T(8,128)S(1)} %fusion.21, s32[8]{0:T(128)S(1)} %copy-done.3), kind=kOutput, calls=%fused_computation.29 | convolution fusion | flops 71303296 | bytes 16810016 | tf_op jit(solution)/shard_map/ob,bnd->ond/dot_general | solution.py:22
  45.5 11.3 %copy.16 = bf16[16,256,1024]{2,1,0:T(8,128)(2,1)} copy(bf16[16,256,1024]{2,0,1:T(8,128)(2,1)} %fusion.16) | data formatting | bytes 16777216 | tf_op jit(solution)/shard_map/ob,bnd->ond/dot_general | solution.py:22
  56.8 7.4 %all-to-all-start.2 = ((bf16[16,256,1024]{2,1,0:T(8,128)(2,1)}), bf16[16,256,1024]{2,1,0:T(8,128)(2,1)}, u32[]{:S(2)}, u32[]{:S(2)}) async-start(bf16[16,256,1024]{2,1,0:T(8,128)(2,1)} %copy.16), calls=%async_computation.2 | async-start | bytes 16777216 | tf_op jit(solution)/shard_map/all_to_all | solution.py:32
  65.2 183.2 %all-to-all-done.2 = bf16[16,256,1024]{2,1,0:T(8,128)(2,1)} async-done(((bf16[16,256,1024]{2,1,0:T(8,128)(2,1)}), bf16[16,256,1024]{2,1,0:T(8,128)(2,1)}, u32[]{:S(2)}, u32[]{:S(2)}) %all-to-all-start.2) | async-done | bytes 8388640 | tf_op jit(solution)/shard_map/all_to_all | solution.py:32
  248.4 192.6 %while.21 = (s32[]{:T(128)}, f32[1,256,1024]{2,1,0:T(8,128)S(1)}, f32[1,256]{1,0:T(1,128)S(1)}, f32[1,1024]{1,0:T(1,128)S(1)}, f32[1]{0:T(128)}, /*index=5*/s32[...) while((s32[]{:T(128)}, f32[1,256,1024]{2,1,0:T(8,128)S(1)}, ...), condition=%wide.region_10.11_spmd.clone, body=%wide.region_3.10_spmd.clone.sunk | while | flops 270928128 | bytes 5274389 | solution.py:75
  254.3 2.2 add_select_fusion.2
  266.4 2.2 add_select_fusion.2
  278.4 2.2 add_select_fusion.2
  287.7 1.4 fusion.34
  290.5 2.2 add_select_fusion.2
  302.5 2.2 add_select_fusion.2
  311.8 1.4 fusion.34
  314.5 2.2 add_select_fusion.2
  326.6 2.2 add_select_fusion.2
  335.9 1.4 fusion.34
  338.6 2.2 add_select_fusion.2
  350.7 2.2 add_select_fusion.2
  360.0 1.4 fusion.34
  362.7 2.2 add_select_fusion.2
  374.7 2.2 add_select_fusion.2
  386.8 2.2 add_select_fusion.2
  398.8 2.2 add_select_fusion.2
  408.1 1.4 fusion.34
  410.9 2.2 add_select_fusion.2
  422.9 2.2 add_select_fusion.2
  434.9 2.2 add_select_fusion.2
  444.0 73.0 %all-reduce.1 = (f32[1,256]{1,0:T(1,128)S(1)}, f32[1,1024]{1,0:T(1,128)S(1)}, f32[1]{0:T(128)}) all-reduce(f32[1,256]{1,0:T(1,128)S(1)} %get-tuple-element.111, f32[1,1024]{1,0:T(1,128)S(1)} %get-tuple-element.112, f32[1]{0:T(128)} %get-tuple-element.113), channel_id=3, replica_groups=mesh['dp'=32,'list'=16] {'dp'}, use_global_device_ids=true, to_apply=%region_12.13.clone | all-reduce | flops 1281 | bytes 10248
  518.4 141.8 %reduce-scatter.3.cloned.1.call-done = f32[1,8,1024]{2,1,0:T(8,128)} async-done(((f32[1,256,1024]{2,1,0:T(8,128)}), f32[1,8,1024]{2,1,0:T(8,128)}) %reduce-scatter.3.cloned.1.call-update) | async-done | bytes 32784 | tf_op jit(solution)/shard_map/reduce_scatter | solution.py:79
  660.1 1.4 add_divide_fusion
  (196 shorter events, 116.2 us)
Async XLA Ops:
  7.2 12.6 %copy-start = (bf16[16,1024]{1,0:T(8,128)(2,1)S(1)}, bf16[16,1024]{1,0:T(8,128)(2,1)}, u32[]{:S(2)}) copy-start(bf16[16,1024]{1,0:T(8,128)(2,1)} %param.18) | copy-start | bytes 98308
  7.2 27.1 %copy-start.3 = (s32[8]{0:T(128)S(1)}, s32[8]{0:T(128)}, u32[]{:S(2)}) copy-start(s32[8]{0:T(128)} %param.16) | copy-start | bytes 100
  8.7 18.4 %all-to-all-start = ((s32[16,1,1]{2,1,0:T(1,128)}), s32[16,1,1]{2,1,0:T(1,128)S(1)}, u32[]{:S(2)}, u32[]{:S(2)}) async-start(s32[16,1,1]{2,1,0:T(1,128)} %copy.13), calls=%async_computation | async-start | bytes 16384 | tf_op jit(solution)/shard_map/all_to_all | solution.py:33
  27.1 29.7 %all-to-all-start.1 = ((s32[16,1,1]{2,1,0:T(1,128)}), s32[16,1,1]{2,1,0:T(1,128)S(1)}, u32[]{:S(2)}, u32[]{:S(2)}) async-start(s32[16,1,1]{2,1,0:T(1,128)} %copy.14), calls=%async_computation.1 | async-start | bytes 16384 | tf_op jit(solution)/shard_map/all_to_all | solution.py:34
  56.8 7.5 %copy-start.2 = (bf16[1,256,1024]{2,1,0:T(8,128)(2,1)S(1)}, bf16[1,256,1024]{2,1,0:T(8,128)(2,1)}, u32[]{:S(2)}) copy-start(bf16[1,256,1024]{2,1,0:T(8,128)(2,1)} %param.19) | copy-start | bytes 1572868
  56.8 191.7 %all-to-all-start.2 = ((bf16[16,256,1024]{2,1,0:T(8,128)(2,1)}), bf16[16,256,1024]{2,1,0:T(8,128)(2,1)}, u32[]{:S(2)}, u32[]{:S(2)}) async-start(bf16[16,256,1024]{2,1,0:T(8,128)(2,1)} %copy.16), calls=%async_computation.2 | async-start | bytes 16777216 | tf_op jit(solution)/shard_map/all_to_all | solution.py:32
  64.2 595.9 %reduce-scatter.3.cloned.1.call-start = ((), (), s32[]{:S(2)}) async-start(), calls=%async_computation.4 | async-start | bytes 1081344 | tf_op jit(solution)/shard_map/reduce_scatter | solution.py:79
  441.1 1.0 copy-start.1
Sparse Core Ops, SparseCore 0:
  442.2 217.8 reduce-scatter.2
where the time goes:
time: 672 us; the launch traced here: 668 us
  waiting for transfers between devices  325 us (48%)
  other arithmetic  85 us (13%)
  blocking collectives  73 us (11%)
  matrix products  69.6 us (10%)
  loops' own time  41.2 us (6%)
  local copies, waits for them, and re-layouts  34.1 us (5%)
  starting transfers between devices  25.1 us (4%)
  between operations  15.4 us (2%)
    all_to_all x1, waiting for transfers between devices, per_device(): lax.all_to_all(outgoing, 'list', split_axis=0, concat_axis=0, tiled=True)  183 us
    reduce_scatter x1, waiting for transfers between devices, per_device(): lax.psum_scatter(fine_sums, 'dp', scatter_dimension=1, tiled=True)  142 us
    unnamed x1, blocking collectives  73 us
    another operation x1, loops' own time, per_device(): carry, _ = lax.scan(visit, start, (arrived, local_slot, in_rows))  41.2 us
    dot_general x16, matrix products, absorb(): jnp.einsum('nk,nd->kd', weight_half, resid_slot, preferred_element_type=j...  35.2 us
    another operation x32, other arithmetic  22.9 us
    dot_general x16, matrix products, absorb(): jnp.einsum('nd,kd->nk', resid_slot, group_centroid_matrix, preferred_elem...  22.4 us
    reduce_sum x16, other arithmetic, absorb(): jnp.sum(jnp.where(live_mask[:, None], resid_slot.astype(jnp.float32), 0.0...  19.6 us
  transfers between devices with their start and end apart: 4, of which 2 were waited for; matrix products, arithmetic and copies ran while one was open for 5% of the time, Pallas kernels for 0%

commit v1 on v0

v1 whole, which is shorter than its diff:
```python
import functools

import jax
import jax.numpy as jnp
from jax import lax
from jax.experimental import pallas as pl
from jax.experimental.pallas import tpu as pltpu
from jax.sharding import PartitionSpec as P

NX, NY, NZ = 4, 8, 8
D, K, B = 1024, 256, 256
SLOTS = 8
OFF = (0, 1, -1, 2, -2, 3, -3, 4)
GROUPS = ((0,), (1, 2), (3, 4), (5, 6), (7,))
AZ0, AZN = 0, 384
AY0, AYN = 384, 256
AX0, AXN = 640, 384
YC, XC = 640, 384
NSEM = 400
RING_AG = (1, 2, 3)
RING_RS = (0, 1, 2, 3)
MESH = pl.DeviceIdType.MESH
BF, F32 = jnp.bfloat16, jnp.float32


def kernel(clus, rows, points, coarse, fine, out, shift,
           pts, res, stage, tab, py, px, ry, rx, szy, szx, rzy, rzx, accy, accx, rfy, rfx,
           rowmsg, rowin, aux, raz, ray, rax, ssem, rsem, lsem):
    dp, li = lax.axis_index("dp"), lax.axis_index("list")
    x, y, z, core = dp // NY, dp % NY, li // 2, li % 2

    def at(dx=0, dy=0, dz=0, dc=0):
        xx = lax.rem(x + dx + NX, NX)
        yy = lax.rem(y + dy + NY, NY)
        zz = lax.rem(z + dz + NZ, NZ)
        return (xx * NY + yy, zz * 2 + lax.rem(core + dc, 2))

    load_pts = pltpu.make_async_copy(points, pts, lsem.at[0])
    load_pts.start()
    load_fine = pltpu.make_async_copy(fine.at[0], tab.at[0], lsem.at[1])
    load_fine.start()

    partners = [dict(dc=1)]
    partners += [dict(dz=d) for d in range(1, NZ)]
    partners += [dict(dy=d) for d in range(1, NY)]
    partners += [dict(dx=d) for d in range(1, NX)]
    barrier = pltpu.get_barrier_semaphore()
    for p in partners:
        pl.semaphore_signal(barrier, inc=1, device_id=at(**p), device_id_type=MESH)

    started = []
    made = {}

    def send(key, src, dst, **to):
        i = len(made)
        c = pltpu.make_async_remote_copy(
            src_ref=src, dst_ref=dst, send_sem=ssem.at[i], recv_sem=rsem.at[i],
            device_id=at(**to), device_id_type=MESH)
        assert key not in made
        made[key] = c
        c.start()
        started.append(c)

    def got(key):
        made[key].wait_recv()

    def got_all(keys):
        for k in keys:
            got(k)

    events = []

    def ev(t, fn, *a):
        events.append((t, len(events), fn, a))

    cents = coarse[...].astype(F32)
    crow = lax.broadcasted_iota(jnp.int32, (16, 1), 0)

    def find(s, parity):
        c = 2 * lax.rem(z + OFF[s] + NZ, NZ) + parity
        b, n = jnp.int32(0), jnp.int32(0)
        for j in range(8):
            hit = clus[j] == c
            b = jnp.where(hit, j, b)
            n = jnp.where(hit, rows[j], n)
        centre = jnp.sum(jnp.where(crow == c, cents, 0.0), axis=0, keepdims=True)
        return b, n, centre

    def residual(s, parity, put):
        b, n, centre = find(s, parity)

        @pl.loop(0, B, step=32)
        def _(r):
            r = pl.multiple_of(r, 32)
            v = pts[b, pl.ds(r, 32), :].astype(F32) - centre
            put[pl.ds(r, 32), :] = v.astype(BF)

        return n

    own_rows = {}

    def send_rows():
        sub = lax.broadcasted_iota(jnp.int32, (8, 128), 0)
        m = jnp.zeros((8, 128), jnp.int32)
        for s in range(SLOTS):
            m = jnp.where(sub == s, find(s, 1 - core)[1], m)
        rowmsg[...] = m
        send("rows", rowmsg, rowin, dc=1)

    def stage_slot(s):
        residual(s, 1 - core, stage.at[s])
        send(("res", s), stage.at[s], res.at[s, pl.ds(B, B)], dc=1)

    def keep_slot(s):
        own_rows[s] = residual(s, core, res.at[s, pl.ds(0, B)])

    def zpieces(s, part):
        h = 2 if part is not None else 1
        q = part or 0
        return (
            ("x", pl.multiple_of(64 * x + q * 32, 32), 64 // h, AX0, AXN),
            ("y", pl.multiple_of(32 * y + q * 16, 16), 32 // h, AY0, AYN),
            ("z", q * 128, 256 // h, AZ0, AZN),
        )

    def zsend(d, way, names):
        s = 0 if d == 1 else OFF.index(way * (d - 1))
        t = 7 if d == 4 else OFF.index(way * d)
        part = None if d < 4 else (0 if way > 0 else 1)
        for name, r0, nr, c0, nc in zpieces(s, part):
            if name in names:
                send(("az", d, way, name), tab.at[s, pl.ds(r0, nr), pl.ds(c0, nc)],
                     tab.at[t, pl.ds(r0, nr), pl.ds(c0, nc)], dz=-way)

    def zhop(d, names):
        for way in (1, -1):
            got_all([("az", d, way, n) for n in names])
            if d < 4:
                zsend(d + 1, way, names)

    def xpiece(s):
        p = tab.at[s, pl.ds(pl.multiple_of(64 * x, 64), 64), pl.ds(AX0, AXN)]
        for j in (2, 1, 3):
            send(("ax", s, j), p, p, dx=j)

    def ydirect(s):
        p = tab.at[s, pl.ds(pl.multiple_of(32 * y, 32), 32), pl.ds(AY0, AYN)]
        for j in (4, 3, 5, 2, 6, 1, 7):
            send(("ayd", s, j), p, p, dy=j)

    def yring(g, h):
        for way in (1, -1):
            sl = GROUPS[g]
            if h == 4:
                sl = sl[:1] if way > 0 else sl[1:]
            if not sl:
                continue
            r0 = pl.multiple_of(32 * lax.rem(y - way * (h - 1) + NY, NY), 32)
            p = tab.at[pl.ds(sl[0], len(sl)), pl.ds(r0, 32), pl.ds(AY0, AYN)]
            send(("ay", g, h, way), p, p, dy=way)

    def yhop(g, h):
        got_all([k for k in (("ay", g, h, 1), ("ay", g, h, -1)) if k in made])
        if h < 4:
            yring(g, h + 1)

    lane = lax.broadcasted_iota(jnp.int32, (1, 128), 1)

    def compute(s):
        r = res.at[s]
        f = tab[s]
        st = lax.dot_general(f, r[...], (((1,), (1,)), ((), ())), preferred_element_type=F32)
        ff = f.astype(F32)
        norm = jnp.sum(ff * ff, axis=1, keepdims=True)
        logits = st * (2.0 / 32.0) - norm * (1.0 / 32.0)
        e = jnp.exp(logits - jnp.max(logits, axis=0, keepdims=True))
        n = own_rows[s]
        n2 = rowin[pl.ds(s, 1), :]
        live = jnp.concatenate([lane < n, lane + 128 < n, lane < n2, lane + 128 < n2], axis=1)
        live = jnp.where(live, 1.0, 0.0)
        w = e * (live / jnp.sum(e, axis=0, keepdims=True))
        wh = w.astype(BF)
        ones = jnp.ones((16, 2 * B), BF)
        cnt = lax.dot_general(ones, wh, (((1,), (1,)), ((), ())), preferred_element_type=F32)
        lhs = jnp.concatenate([wh, jnp.broadcast_to(live, (16, 2 * B)).astype(BF)], axis=0)
        sub = lax.broadcasted_iota(jnp.int32, (8, 128), 0)
        drift = jnp.zeros((8, 128), F32)
        for c0 in range(0, D, 128):
            p = jnp.dot(lhs, r[:, c0:c0 + 128], preferred_element_type=F32)
            drift = jnp.where(sub == c0 // 128, p[K:K + 8], drift)
            if c0 < YC:
                for yy in range(NY):
                    q = jnp.concatenate([p[64 * k + 8 * yy:64 * k + 8 * yy + 8] for k in range(NX)], axis=0)
                    py[s, yy, :, c0:c0 + 128] = q.astype(BF)
            else:
                for xx in range(NX):
                    px[s, xx, :, c0 - YC:c0 - YC + 128] = p[64 * xx:64 * xx + 64].astype(BF)
        seen = jnp.broadcast_to((n + n2).astype(F32), (8, 128))
        more = jnp.where(sub == 0, cnt[:8, :128], jnp.where(sub == 1, cnt[:8, 128:], seen))
        aux[s, 0:8, :] = drift
        aux[s, 8:16, :] = more
        if s:
            send(("auxz", s), aux.at[s], raz.at[s], dz=OFF[s])

    def rs_x(s):
        for j in (2, 1, 3):
            send(("rx", s, j), px.at[s, lax.rem(x + j, NX)], rx.at[s, j - 1], dx=j)

    def rs_x_done(s):
        got_all([("rx", s, j) for j in (1, 2, 3)])
        v = px[s, x].astype(F32)
        for j in range(3):
            v = v + rx[s, j].astype(F32)
        if s == 0:
            accx[...] = v.reshape(NY, 8, XC)
        else:
            szx[s] = v.astype(BF)
            send(("zx", s), szx.at[s], rzx.at[s], dz=OFF[s])

    def rs_y_send(g, dist):
        for way in (1, -1):
            sl = GROUPS[g]
            if dist == 4:
                sl = sl[:1] if way > 0 else sl[1:]
            if not sl:
                continue
            to = lax.rem(y + way * dist + NY, NY)
            send(("ry", g, dist, way), py.at[pl.ds(sl[0], len(sl)), to],
                 ry.at[(way < 0) * 4 + dist - 1, pl.ds(sl[0], len(sl))], dy=way)

    def rs_y_hop(g, dist):
        for way in (1, -1):
            if ("ry", g, dist, way) not in made:
                continue
            sl = GROUPS[g]
            if dist == 4:
                sl = sl[:1] if way > 0 else sl[1:]
            got(("ry", g, dist, way))
            to = lax.rem(y + way * (dist - 1) + NY, NY)
            for s in sl:
                v = py[s, to].astype(F32) + ry[(way < 0) * 4 + dist - 1, s].astype(F32)
                py[s, to] = v.astype(BF)
        rs_y_send(g, dist - 1)

    def rs_y_out(s, v):
        if s == 0:
            accy[...] = v.reshape(NX, 8, YC)
        else:
            szy[s] = v.astype(BF)
            send(("zy", s), szy.at[s], rzy.at[s], dz=OFF[s])

    def rs_y_done(g):
        got_all([("ry", g, 1, 1), ("ry", g, 1, -1)])
        for s in GROUPS[g]:
            rs_y_out(s, py[s, y].astype(F32) + ry[0, s].astype(F32) + ry[4, s].astype(F32))

    def rs_y_direct(s):
        for j in (4, 3, 5, 2, 6, 1, 7):
            send(("ryd", s, j), py.at[s, lax.rem(y + j, NY)], ry.at[j - 1, s], dy=j)

    def rs_y_direct_done(s):
        v = py[s, y].astype(F32)
        for j in range(1, 8):
            got(("ryd", s, j))
            v = v + ry[j - 1, s].astype(F32)
        rs_y_out(s, v)

    def add_z(s):
        got(("zy", s))
        accy[...] += rzy[s].astype(F32).reshape(NX, 8, YC)
        got(("zx", s))
        accx[...] += rzx[s].astype(F32).reshape(NY, 8, XC)

    def last_send():
        for j in (2, 1, 3):
            send(("fy", j), accy.at[lax.rem(x + j, NX)], rfy.at[j - 1], dx=j)
        for j in (4, 3, 5, 2, 6, 1, 7):
            send(("fx", j), accx.at[lax.rem(y + j, NY)], rfx.at[j - 1], dy=j)

    def aux_z():
        v = aux[0]
        for s in range(1, SLOTS):
            got(("auxz", s))
            v = v + raz[s]
        raz[0] = v
        ray[y] = v
        for j in (4, 3, 5, 2, 6, 1, 7):
            send(("auxy", j), raz.at[0], ray.at[y], dy=j)

    def aux_y():
        got_all([("auxy", j) for j in range(1, NY)])
        v = ray[0]
        for j in range(1, NY):
            v = v + ray[j]
        aux[0] = v
        rax[x] = v
        for j in (2, 1, 3):
            send(("auxx", j), aux.at[0], rax.at[x], dx=j)

    def aux_x():
        got_all([("auxx", j) for j in range(1, NX)])
        v = rax[0]
        for j in range(1, NX):
            v = v + rax[j]
        seen = v[10:11, :]
        d = v[0:8] / (seen + 1.0)
        for i in range(8):
            shift[:, 128 * i:128 * i + 128] = d[i:i + 1]
        k0 = lax.rem(dp, 16) * 8
        line = jnp.where(dp < 16, v[8:9], v[9:10])
        pick = lax.broadcasted_iota(jnp.int32, (8, 128), 1) == k0 + lax.broadcasted_iota(jnp.int32, (8, 128), 0)
        made["cnt"] = jnp.sum(jnp.where(pick, jnp.broadcast_to(line, (8, 128)), 0.0), axis=1, keepdims=True)

    def finish():
        old = tab[0, pl.ds(pl.multiple_of((dp // 2) * 16, 16), 16), :].astype(F32)
        old = jnp.where(lax.rem(dp, 2) == 0, old[:8], old[8:])
        vy = accy[x]
        for j in (1, 2, 3):
            got(("fy", j))
            vy = vy + rfy[j - 1]
        div = made["cnt"] + 1.0
        out[0, :, :YC] = (vy + old[:, :YC]) / div
        vx = accx[y]
        for j in range(1, NY):
            got(("fx", j))
            vx = vx + rfx[j - 1]
        out[0, :, YC:] = (vx + old[:, YC:]) / div

    hz, hzz, hx, hy, hr = 3.2, 4.2, 4.0, 2.3, 2.7
    for way in (1, -1):
        ev(0.0, zsend, 1, way, "xy")
    for way in (1, -1):
        ev(0.01, zsend, 1, way, "z")
    ev(0.05, load_pts.wait)
    ev(0.1, send_rows)
    for s in range(SLOTS):
        ev(0.2 + 0.7 * s, stage_slot, s)
        ev(0.5 + 0.7 * s, keep_slot, s)
    ready = {0: 2.6}
    for d in range(1, 5):
        g = d
        ev(hz * d, zhop, d, "xy")
        ev(max(hzz * d, hz * d + 0.1), zhop, d, "z")
        for s in GROUPS[g]:
            ev(hz * d + 0.01, xpiece, s)
            ev(hz * d + hx, got_all, [("ax", s, j) for j in (1, 2, 3)])
        if g in RING_AG:
            ev(hz * d + 0.02, yring, g, 1)
            for h in range(1, 5):
                ev(hz * d + hy * h, yhop, g, h)
            ready[g] = max(hz * d + hy * 4, hzz * d, hz * d + hx) + 0.02
        else:
            for s in GROUPS[g]:
                ev(hz * d + 0.02, ydirect, s)
                ev(hz * d + 5.0, got_all, [("ayd", s, j) for j in range(1, 8)])
            ready[g] = max(hz * d + 5.0, hzz * d, hz * d + hx) + 0.02
    busy = 0.0
    last = 0.0
    for g in range(5):
        t = max(ready[g], busy)
        for s in GROUPS[g]:
            if s == 0:
                ev(t - 0.01, got, "rows")
            ev(t, got, ("res", s))
            ev(t, compute, s)
            t += 1.0
            ev(t, rs_x, s)
        busy = t
        if g in RING_RS:
            ev(t, rs_y_send, g, 4)
            for dist in range(4, 1, -1):
                if dist == 4:
                    ev(t + hr, rs_y_hop, g, 4)
                else:
                    ev(t + hr * (5 - dist), rs_y_hop, g, dist)
            ev(t + hr * 4, rs_y_done, g)
            tz = t + hr * 4
        else:
            for s in GROUPS[g]:
                ev(t + 0.01, rs_y_direct, s)
                ev(t + 6.0, rs_y_direct_done, s)
            tz = t + 6.0
        for s in GROUPS[g]:
            ev(t + 4.0, rs_x_done, s)
            if s:
                ev(max(tz, last) + 4.2, add_z, s)
        last = max(last, tz)
    ev(busy + 4.0, aux_z)
    ev(busy + 8.0, aux_y)
    ev(busy + 11.0, aux_x)
    ev(last + 4.6, last_send)
    ev(last + 8.0, finish)

    load_fine.wait()
    pl.semaphore_wait(barrier, len(partners))
    for _, _, fn, a in sorted(events, key=lambda e: e[:2]):
        fn(*a)
    for c in started:
        c.wait_send()


def per_device(points, block_cluster, block_rows, coarse, fine):
    vmem = pl.BlockSpec(memory_space=pltpu.VMEM)
    smem = pl.BlockSpec(memory_space=pltpu.SMEM)
    hbm = pl.BlockSpec(memory_space=pl.ANY)
    return pl.pallas_call(
        kernel,
        out_shape=(jax.ShapeDtypeStruct((1, 8, D), F32), jax.ShapeDtypeStruct((1, D), F32)),
        in_specs=[smem, smem, hbm, vmem, hbm],
        out_specs=(vmem, vmem),
        scratch_shapes=[
            pltpu.VMEM((8, B, D), BF),
            pltpu.VMEM((SLOTS, 2 * B, D), BF),
            pltpu.VMEM((SLOTS, B, D), BF),
            pltpu.VMEM((SLOTS, K, D), BF),
            pltpu.VMEM((SLOTS, NY, 32, YC), BF),
            pltpu.VMEM((SLOTS, NX, 64, XC), BF),
            pltpu.VMEM((8, SLOTS, 32, YC), BF),
            pltpu.VMEM((SLOTS, 3, 64, XC), BF),
            pltpu.VMEM((SLOTS, 32, YC), BF),
            pltpu.VMEM((SLOTS, 64, XC), BF),
            pltpu.VMEM((SLOTS, 32, YC), BF),
            pltpu.VMEM((SLOTS, 64, XC), BF),
            pltpu.VMEM((NX, 8, YC), F32),
            pltpu.VMEM((NY, 8, XC), F32),
            pltpu.VMEM((NX - 1, 8, YC), F32),
            pltpu.VMEM((NY - 1, 8, XC), F32),
            pltpu.VMEM((8, 128), jnp.int32),
            pltpu.VMEM((8, 128), jnp.int32),
            pltpu.VMEM((SLOTS, 16, 128), F32),
            pltpu.VMEM((SLOTS, 16, 128), F32),
            pltpu.VMEM((NY, 16, 128), F32),
            pltpu.VMEM((NX, 16, 128), F32),
            pltpu.SemaphoreType.DMA((NSEM,)),
            pltpu.SemaphoreType.DMA((NSEM,)),
            pltpu.SemaphoreType.DMA((2,)),
        ],
        compiler_params=pltpu.CompilerParams(
            collective_id=0, has_side_effects=True, vmem_limit_bytes=56 * 1024 * 1024),
        cost_estimate=pl.CostEstimate(flops=8 * 10**9, bytes_accessed=5 * 10**6, transcendentals=10**6),
        name="lloyd",
    )(block_cluster, block_rows, points.reshape(8, B, D), coarse, fine)


def solution(mesh):
    placed = (
        P(("dp", "list"), None),
        P(("dp", "list")),
        P(("dp", "list")),
        P(),
        P("list", None, None),
    )
    return jax.shard_map(
        per_device,
        mesh=mesh,
        in_specs=placed,
        out_specs=(P("list", "dp", None), P("list", None)),
        check_vma=False,
    )
```

time: 672 us -> 97.4 us (0.14)
  the two profiles are of different devices: /device:TPU:16 before, /device:TPU:8 now
where the time goes in v1:
time: 97.4 us; the launch traced here: 97.1 us
  Pallas kernels  93.8 us (96%)
  local copies, waits for them, and re-layouts  2.65 us (3%)
    pallas_call x1, Pallas kernels, per_device(): pl.pallas_call(kernel, out_shape=(jax.ShapeDtypeStruct((1, 8, D), F32), j...  93.8 us
    unnamed x2, local copies, waits for them, and re-layouts  2.65 us

profile of v1, /device:TPU:8, one launch (start us, length us, event | category | flops | bytes accessed | tf_op | source)
XLA Modules:
  0.0 97.1 jit_solution(8849395101938624556)
XLA Ops:
  0.6 93.8 %lloyd.1 = (f32[1,8,1024]{2,1,0:T(8,128)}, f32[1,1024]{1,0:T(1,128)}) custom-call(s32[8]{0:T(128)} %clus.1, s32[8]{0:T(128)} %rows.1, bf16[8,256,1024]{2,1,0:T(8,128)(2,1)} %bitcast.1, bf16[16,1024]{1,0:T(8,128)(2,1)} %coarse.1, bf16[1,256,1024]{2,1,0:T(8,128)(2,1)} %fine.1), custom_call_target="tpu_custom_call" | custom-call | flops 8000000000 | bytes 5000000 | tf_op jit(solution)/shard_map/lloyd/pallas_call | solution.py:406
  94.5 1.4 %copy.9 = f32[1,8,1024]{2,1,0:T(8,128)} copy(f32[1,8,1024]{2,1,0:T(8,128)} %get-tuple-element.4) | data formatting | bytes 65536
  95.8 1.3 %copy.10 = f32[1,1024]{1,0:T(1,128)} copy(f32[1,1024]{1,0:T(1,128)} %get-tuple-element.5) | data formatting | bytes 8192

commit v2 on v1

v2 whole, which is shorter than its diff:
```python
import functools

import jax
import jax.numpy as jnp
from jax import lax
from jax.experimental import pallas as pl
from jax.experimental.pallas import tpu as pltpu
from jax.sharding import PartitionSpec as P

NX, NY, NZ = 4, 8, 8
D, K, B = 1024, 256, 256
SLOTS = 8
OFF = (0, 1, -1, 2, -2, 3, -3, 4)
GROUPS = ((0,), (1, 2), (3, 4), (5, 6), (7,))
AZ0, AZN = 0, 512
AX0, AXN = 512, 512
FAR = (5, 6, 7)
H = D // 2
NSEM = 400
MESH = pl.DeviceIdType.MESH
BF, F32 = jnp.bfloat16, jnp.float32
ORDER = (
    ("zs", 1, -1, "x"), ("zs", 1, 1, "x"), ("zs", 1, -1, 0), ("zs", 1, 1, 0), ("zs", 1, 1, 1), ("zs", 1, -1, 1),
    ("pts",), ("stage", 0), ("stage", 1), ("keep", 0), ("keep", 1), ("stage", 2), ("stage", 3), ("keep", 2),
    ("keep", 3), ("stage", 4), ("stage", 5), ("xp", 1), ("zf", 1, -1, "x"), ("zf", 1, 1, "x"), ("keep", 4),
    ("keep", 5), ("stage", 6), ("stage", 7), ("keep", 6), ("keep", 7), ("zf", 1, -1, 0), ("zf", 1, 1, 0), ("comp", 0),
    ("ry", 0, 4), ("xp", 2), ("zf", 1, -1, 1), ("zf", 1, 1, 1), ("comp", 1), ("xp", 3), ("xp", 4), ("zf", 2, -1, "x"),
    ("zf", 2, 1, "x"), ("ry", 0, 3), ("zf", 2, -1, 0), ("zf", 2, 1, 0), ("comp", 2), ("ry", 1, 4), ("zf", 2, 1, 1),
    ("zf", 2, -1, 1), ("ry", 0, 2), ("zf", 3, 1, "x"), ("xp", 5), ("zf", 3, -1, "x"), ("xp", 6), ("comp", 3),
    ("ry", 1, 3), ("zf", 3, -1, 0), ("zf", 3, 1, 0), ("comp", 4), ("ry", 0, 1), ("ry", 2, 4), ("zf", 3, -1, 1),
    ("zf", 3, 1, 1), ("xp", 7), ("comp", 5), ("ry", 1, 2), ("comp", 6), ("ryd", 0), ("ry", 2, 3), ("comp", 7),
    ("ry", 1, 1), ("ry", 2, 2), ("rxd", 5), ("auxz",), ("ryd", 1), ("ry", 2, 1), ("rxd", 6), ("addz", 2), ("addz", 1),
    ("bdone", 5), ("auxy",), ("rxd", 7), ("ryd", 2), ("auxx",), ("bdone", 6), ("addz", 4), ("addz", 3), ("last",),
    ("bdone", 7), ("finish",),
)

def kernel(clus, rows, points, coarse, fine, out,
           pts, res, stage, tab, py, px, ry, rx, szy, rzy, sbx, rbx, szc, rzc, accy, rfy,
           rowmsg, rowin, aux, raz, ray, rax, ssem, rsem, lsem):
    dp, li = lax.axis_index("dp"), lax.axis_index("list")
    x, y, z, core = dp // NY, dp % NY, li // 2, li % 2

    def at(dx=0, dy=0, dz=0, dc=0):
        xx = lax.rem(x + dx + NX, NX)
        yy = lax.rem(y + dy + NY, NY)
        zz = lax.rem(z + dz + NZ, NZ)
        return (xx * NY + yy, zz * 2 + lax.rem(core + dc, 2))

    load_pts = pltpu.make_async_copy(points, pts, lsem.at[0])
    load_pts.start()
    load_fine = pltpu.make_async_copy(fine.at[0], tab.at[0], lsem.at[1])
    load_fine.start()

    partners = [dict(dc=1)]
    partners += [dict(dz=d) for d in range(1, NZ)]
    partners += [dict(dy=d) for d in range(1, NY)]
    partners += [dict(dx=d) for d in range(1, NX)]
    barrier = pltpu.get_barrier_semaphore()
    for p in partners:
        pl.semaphore_signal(barrier, inc=1, device_id=at(**p), device_id_type=MESH)

    started = []
    made = {}
    sent = 0

    def send(key, src, dst, **to):
        i = len(made)
        c = pltpu.make_async_remote_copy(
            src_ref=src, dst_ref=dst, send_sem=ssem.at[i], recv_sem=rsem.at[i],
            device_id=at(**to), device_id_type=MESH)
        assert key not in made
        made[key] = c
        c.start()
        started.append(c)

    waited = set()

    def got(key):
        if key not in waited:
            waited.add(key)
            made[key].wait_recv()

    def got_all(keys):
        for k in keys:
            got(k)

    def group_of(s):
        return [s in g for g in GROUPS].index(True)

    cents = coarse[...].astype(F32)
    crow = lax.broadcasted_iota(jnp.int32, (16, 1), 0)

    def find(s, parity):
        c = 2 * lax.rem(z + OFF[s] + NZ, NZ) + parity
        b, n = jnp.int32(0), jnp.int32(0)
        for j in range(8):
            hit = clus[j] == c
            b = jnp.where(hit, j, b)
            n = jnp.where(hit, rows[j], n)
        centre = jnp.sum(jnp.where(crow == c, cents, 0.0), axis=0, keepdims=True)
        return b, n, centre

    def residual(s, parity, put):
        b, n, centre = find(s, parity)

        @pl.loop(0, B, step=32)
        def _(r):
            r = pl.multiple_of(r, 32)
            v = pts[b, pl.ds(r, 32), :].astype(F32) - centre
            put[pl.ds(r, 32), :] = v.astype(BF)

        return n

    own_rows = {}

    def send_rows():
        sub = lax.broadcasted_iota(jnp.int32, (8, 128), 0)
        m = jnp.zeros((8, 128), jnp.int32)
        for s in range(SLOTS):
            m = jnp.where(sub == s, find(s, 1 - core)[1], m)
        rowmsg[...] = m
        send("rows", rowmsg, rowin, dc=1)

    def stage_slot(s):
        residual(s, 1 - core, stage.at[s])
        send(("res", s), stage.at[s], res.at[s, pl.ds(B, B)], dc=1)

    def keep_slot(s):
        own_rows[s] = residual(s, core, res.at[s, pl.ds(0, B)])

    def zsend(d, way, name):
        s = 0 if d == 1 else OFF.index(way * (d - 1))
        t = 7 if d == 4 else OFF.index(way * d)
        if name == "x":
            half = 32 if d == 4 and way < 0 else 0
            r0, nr, c0, nc = pl.multiple_of(64 * x + half, 32), 32 if d == 4 else 64, AX0, AXN
        else:
            if d == 4 and (name == 0) != (way > 0):
                return
            r0, nr, c0, nc = 128 * name, 128, AZ0, AZN
        send(("az", d, way, name), tab.at[s, pl.ds(r0, nr), pl.ds(c0, nc)],
             tab.at[t, pl.ds(r0, nr), pl.ds(c0, nc)], dz=-way)

    def zhop(d, way, name):
        got(("az", d, way, name))
        zsend(d + 1, way, name)

    def znear(s, name):
        if s == 7:
            got_all([("az", 4, way, name) for way in (1, -1) if ("az", 4, way, name) in made])
        else:
            got(("az", abs(OFF[s]), 1 if OFF[s] > 0 else -1, name))

    def xdirect(s):
        znear(s, "x")
        p = tab.at[s, pl.ds(pl.multiple_of(64 * x, 64), 64), pl.ds(AX0, AXN)]
        for j in (2, 1, 3):
            send(("ax", s, j), p, p, dx=j)

    def table_ready(s):
        if s == 0:
            return
        znear(s, 0)
        znear(s, 1)
        got_all([("ax", s, j) for j in (1, 2, 3)])

    lane = lax.broadcasted_iota(jnp.int32, (1, 128), 1)

    def compute(s):
        table_ready(s)
        if s == 0:
            got("rows")
        got(("res", s))
        r = res.at[s]
        f = tab[s]
        st = lax.dot_general(f, r[...], (((1,), (1,)), ((), ())), preferred_element_type=F32)
        ff = f.astype(F32)
        norm = jnp.sum(ff * ff, axis=1, keepdims=True)
        logits = st * (2.0 / 32.0) - norm * (1.0 / 32.0)
        e = jnp.exp(logits - jnp.max(logits, axis=0, keepdims=True))
        n = own_rows[s]
        n2 = rowin[pl.ds(s, 1), :]
        live = jnp.concatenate([lane < n, lane + 128 < n, lane < n2, lane + 128 < n2], axis=1)
        live = jnp.where(live, 1.0, 0.0)
        w = e * (live / jnp.sum(e, axis=0, keepdims=True))
        wh = w.astype(BF)
        ones = jnp.ones((16, 2 * B), BF)
        cnt = lax.dot_general(ones, wh, (((1,), (1,)), ((), ())), preferred_element_type=F32)
        lhs = jnp.concatenate([wh, jnp.broadcast_to(live, (16, 2 * B)).astype(BF)], axis=0)
        sub = lax.broadcasted_iota(jnp.int32, (8, 128), 0)
        drift = jnp.zeros((8, 128), F32)
        for c0 in range(0, D, 128):
            p = jnp.dot(lhs, r[:, c0:c0 + 128], preferred_element_type=F32)
            drift = jnp.where(sub == c0 // 128, p[K:K + 8], drift)
            if s not in FAR:
                for yy in range(NY):
                    q = jnp.concatenate([p[64 * k + 8 * yy:64 * k + 8 * yy + 8] for k in range(NX)], axis=0)
                    py[s, yy, :, c0:c0 + 128] = q.astype(BF)
            else:
                for xx in range(NX):
                    px[s - FAR[0], xx, :, c0:c0 + 128] = p[64 * xx:64 * xx + 64].astype(BF)
        seen = jnp.broadcast_to((n + n2).astype(F32), (8, 128))
        more = jnp.where(sub == 0, cnt[:8, :128], jnp.where(sub == 1, cnt[:8, 128:], seen))
        aux[s, 0:8, :] = drift
        aux[s, 8:16, :] = more
        if s:
            send(("auxz", s), aux.at[s], raz.at[s], dz=OFF[s])
        if s in FAR:
            rs_x(s - FAR[0])

    def rs_x(f):
        for j in (2, 1, 3):
            send(("rx", f, j), px.at[f, lax.rem(x + j, NX)], rx.at[f, j - 1], dx=j)

    def rs_x_done(f):
        v = px[f, x].astype(F32)
        for j in (1, 3, 2):
            got(("rx", f, j))
            v = v + rx[f, j - 1].astype(F32)
        for yy in range(NY):
            w = v[8 * yy:8 * yy + 8]
            sbx[f, yy] = jnp.concatenate([w[:, :H], w[:, H:]], axis=0).astype(BF)
        for j in (4, 3, 5, 2, 6, 1, 7):
            send(("bx", f, j), sbx.at[f, lax.rem(y + j, NY)], rbx.at[f, j - 1], dy=j)

    def rs_far_done(f):
        v = sbx[f, y].astype(F32)
        for j in range(1, NY):
            got(("bx", f, j))
            v = v + rbx[f, j - 1].astype(F32)
        szc[f] = v
        send(("zc", f), szc.at[f], rzc.at[f], dz=OFF[f + FAR[0]])

    def rs_y_send(g, dist):
        for way in (1, -1):
            sl = GROUPS[g]
            if dist == 4:
                sl = sl[:1] if way > 0 else sl[1:]
            if not sl:
                continue
            to = lax.rem(y + way * dist + NY, NY)
            send(("ry", g, dist, way), py.at[pl.ds(sl[0], len(sl)), to],
                 ry.at[(way < 0) * 4 + dist - 1, pl.ds(sl[0], len(sl))], dy=way)

    def rs_y_hop(g, dist):
        for way in (1, -1):
            if ("ry", g, dist, way) not in made:
                continue
            sl = GROUPS[g]
            if dist == 4:
                sl = sl[:1] if way > 0 else sl[1:]
            got(("ry", g, dist, way))
            to = lax.rem(y + way * (dist - 1) + NY, NY)
            for s in sl:
                v = py[s, to].astype(F32) + ry[(way < 0) * 4 + dist - 1, s].astype(F32)
                py[s, to] = v.astype(BF)
        rs_y_send(g, dist - 1)

    def rs_y_out(s, v):
        if s == 0:
            accy[...] = v.reshape(NX, 8, D)
        else:
            szy[s] = v.astype(BF)
            send(("zy", s), szy.at[s], rzy.at[s], dz=OFF[s])

    def rs_y_done(g):
        got_all([("ry", g, 1, 1), ("ry", g, 1, -1)])
        for s in GROUPS[g]:
            rs_y_out(s, py[s, y].astype(F32) + ry[0, s].astype(F32) + ry[4, s].astype(F32))

    def add_z(s):
        got(("zy", s))
        accy[...] += rzy[s].astype(F32).reshape(NX, 8, D)

    def last_send():
        for j in (2, 1, 3):
            send(("fy", j), accy.at[lax.rem(x + j, NX)], rfy.at[j - 1], dx=j)

    def aux_z():
        v = aux[0]
        for s in range(1, SLOTS):
            got(("auxz", s))
            v = v + raz[s]
        raz[0] = v
        ray[y] = v
        for j in (4, 3, 5, 2, 6, 1, 7):
            send(("auxy", j), raz.at[0], ray.at[y], dy=j)

    def aux_y():
        got_all([("auxy", j) for j in range(1, NY)])
        v = ray[0]
        for j in range(1, NY):
            v = v + ray[j]
        aux[0] = v
        rax[x] = v
        for j in (2, 1, 3):
            send(("auxx", j), aux.at[0], rax.at[x], dx=j)

    def aux_x():
        got_all([("auxx", j) for j in range(1, NX)])
        v = rax[0]
        for j in range(1, NX):
            v = v + rax[j]
        seen = v[10:11, :]
        d = v[0:8] / (seen + 1.0)
        for i in range(8):
            out[8:9, 128 * i:128 * i + 128] = d[i:i + 1]
        k0 = lax.rem(dp, 16) * 8
        line = jnp.where(dp < 16, v[8:9], v[9:10])
        pick = lax.broadcasted_iota(jnp.int32, (8, 128), 1) == k0 + lax.broadcasted_iota(jnp.int32, (8, 128), 0)
        made["cnt"] = jnp.sum(jnp.where(pick, jnp.broadcast_to(line, (8, 128)), 0.0), axis=1, keepdims=True)

    def finish():
        nonlocal sent
        sent = len(started) - 8
        for c in started[:sent]:
            c.wait_send()
        old = tab[0, pl.ds(pl.multiple_of((dp // 2) * 16, 16), 16), :].astype(F32)
        old = jnp.where(lax.rem(dp, 2) == 0, old[:8], old[8:])
        v = old + accy[x]
        for j in (1, 3, 2):
            got(("fy", j))
            v = v + rfy[j - 1]
        got(("zc", 0))
        far = rzc[0]
        for f in range(1, len(FAR)):
            got(("zc", f))
            far = far + rzc[f]
        div = made["cnt"] + 1.0
        out[:8, :H] = (v[:, :H] + far[:8]) / div
        out[:8, H:] = (v[:, H:] + far[8:]) / div

    def run(kind, *a):
        if kind == "pts":
            load_pts.wait()
            send_rows()
        elif kind == "zs":
            zsend(*a)
        elif kind == "zf":
            zhop(*a)
        elif kind == "xp":
            xdirect(*a)
        elif kind == "stage":
            stage_slot(*a)
        elif kind == "keep":
            keep_slot(*a)
        elif kind == "comp":
            compute(*a)
        elif kind == "rxd":
            rs_x_done(a[0] - FAR[0])
        elif kind == "bdone":
            rs_far_done(a[0] - FAR[0])
        elif kind == "ry":
            if a[1] == 4:
                rs_y_send(*a)
            else:
                rs_y_hop(a[0], a[1] + 1)
        elif kind == "ryd":
            rs_y_done(*a)
        elif kind == "addz":
            add_z(*a)
        elif kind == "auxz":
            aux_z()
        elif kind == "auxy":
            aux_y()
        elif kind == "auxx":
            aux_x()
        elif kind == "last":
            last_send()
        elif kind == "finish":
            finish()

    load_fine.wait()
    pl.semaphore_wait(barrier, len(partners))
    for e in ORDER:
        run(*e)
    for c in started[sent:]:
        c.wait_send()


def per_device(points, block_cluster, block_rows, coarse, fine):
    vmem = pl.BlockSpec(memory_space=pltpu.VMEM)
    smem = pl.BlockSpec(memory_space=pltpu.SMEM)
    hbm = pl.BlockSpec(memory_space=pl.ANY)
    far, near = len(FAR), SLOTS - len(FAR)
    both = pl.pallas_call(
        kernel,
        out_shape=jax.ShapeDtypeStruct((16, D), F32),
        in_specs=[smem, smem, hbm, vmem, hbm],
        out_specs=vmem,
        scratch_shapes=[
            pltpu.VMEM((8, B, D), BF),
            pltpu.VMEM((SLOTS, 2 * B, D), BF),
            pltpu.VMEM((SLOTS, B, D), BF),
            pltpu.VMEM((SLOTS, K, D), BF),
            pltpu.VMEM((near, NY, 32, D), BF),
            pltpu.VMEM((far, NX, 64, D), BF),
            pltpu.VMEM((8, near, 32, D), BF),
            pltpu.VMEM((far, NX - 1, 64, D), BF),
            pltpu.VMEM((near, 32, D), BF),
            pltpu.VMEM((near, 32, D), BF),
            pltpu.VMEM((far, NY, 16, H), BF),
            pltpu.VMEM((far, NY - 1, 16, H), BF),
            pltpu.VMEM((far, 16, H), F32),
            pltpu.VMEM((far, 16, H), F32),
            pltpu.VMEM((NX, 8, D), F32),
            pltpu.VMEM((NX - 1, 8, D), F32),
            pltpu.VMEM((8, 128), jnp.int32),
            pltpu.VMEM((8, 128), jnp.int32),
            pltpu.VMEM((SLOTS, 16, 128), F32),
            pltpu.VMEM((SLOTS, 16, 128), F32),
            pltpu.VMEM((NY, 16, 128), F32),
            pltpu.VMEM((NX, 16, 128), F32),
            pltpu.SemaphoreType.DMA((NSEM,)),
            pltpu.SemaphoreType.DMA((NSEM,)),
            pltpu.SemaphoreType.DMA((2,)),
        ],
        compiler_params=pltpu.CompilerParams(
            collective_id=0, has_side_effects=True, vmem_limit_bytes=56 * 1024 * 1024),
        cost_estimate=pl.CostEstimate(flops=8 * 10**9, bytes_accessed=5 * 10**6, transcendentals=10**6),
        name="lloyd",
    )(block_cluster, block_rows, points.reshape(8, B, D), coarse, fine)
    return both[:8].reshape(1, 8, D), both[8:9]


def solution(mesh):
    placed = (
        P(("dp", "list"), None),
        P(("dp", "list")),
        P(("dp", "list")),
        P(),
        P("list", None, None),
    )
    return jax.shard_map(
        per_device,
        mesh=mesh,
        in_specs=placed,
        out_specs=(P("list", "dp", None), P("list", None)),
        check_vma=False,
    )
```

time: 97.4 us -> 84.7 us (0.87)
  the two profiles are of different devices: /device:TPU:8 before, /device:TPU:4 now
where the time goes in v2:
time: 84.7 us; the launch traced here: 84.4 us
  Pallas kernels  81.1 us (96%)
  local copies, waits for them, and re-layouts  2.73 us (3%)
    pallas_call x1, Pallas kernels, per_device(): pl.pallas_call(kernel, out_shape=jax.ShapeDtypeStruct((16, D), F32), in_s...  81.1 us

profile of v2, /device:TPU:4, one launch (start us, length us, event | category | flops | bytes accessed | tf_op | source)
XLA Modules:
  0.0 84.4 jit_solution(12384081070255945243)
XLA Ops:
  0.6 81.1 %lloyd.1 = f32[16,1024]{1,0:T(8,128)} custom-call(s32[8]{0:T(128)} %clus.1, s32[8]{0:T(128)} %rows.1, bf16[8,256,1024]{2,1,0:T(8,128)(2,1)} %bitcast.3, bf16[16,1024]{1,0:T(8,128)(2,1)} %coarse.1, bf16[1,256,1024]{2,1,0:T(8,128)(2,1)} %fine.1), custom_call_target="tpu_custom_call" | custom-call | flops 8000000000 | bytes 5000000 | tf_op jit(solution)/shard_map/lloyd/pallas_call | solution.py:386
  81.7 1.4 %slice.7 = f32[1,1024]{1,0:T(1,128)} slice(f32[16,1024]{1,0:T(8,128)} %lloyd.1), slice={[8:9], [0:1024]} | slice | bytes 8192 | tf_op jit(solution)/shard_map/slice | solution.py:423
  83.0 1.4 %slice_bitcast_fusion = f32[1,8,1024]{2,1,0:T(8,128)} fusion(f32[16,1024]{1,0:T(8,128)} %lloyd.1), kind=kLoop, calls=%fused_computation | loop fusion | bytes 65536 | tf_op jit(solution)/shard_map/reshape | solution.py:423

commit v3 on v2

--- a/solution.py
+++ b/solution.py
@@ -16,22 +16,22 @@
 AX0, AXN = 512, 512
 FAR = (5, 6, 7)
 H = D // 2
+EARLY = (0, 1, 2)
 NSEM = 400
 MESH = pl.DeviceIdType.MESH
 BF, F32 = jnp.bfloat16, jnp.float32
 ORDER = (
-    ("zs", 1, -1, "x"), ("zs", 1, 1, "x"), ("zs", 1, -1, 0), ("zs", 1, 1, 0), ("zs", 1, 1, 1), ("zs", 1, -1, 1),
-    ("pts",), ("stage", 0), ("stage", 1), ("keep", 0), ("keep", 1), ("stage", 2), ("stage", 3), ("keep", 2),
-    ("keep", 3), ("stage", 4), ("stage", 5), ("xp", 1), ("zf", 1, -1, "x"), ("zf", 1, 1, "x"), ("keep", 4),
-    ("keep", 5), ("stage", 6), ("stage", 7), ("keep", 6), ("keep", 7), ("zf", 1, -1, 0), ("zf", 1, 1, 0), ("comp", 0),
-    ("ry", 0, 4), ("xp", 2), ("zf", 1, -1, 1), ("zf", 1, 1, 1), ("comp", 1), ("xp", 3), ("xp", 4), ("zf", 2, -1, "x"),
-    ("zf", 2, 1, "x"), ("ry", 0, 3), ("zf", 2, -1, 0), ("zf", 2, 1, 0), ("comp", 2), ("ry", 1, 4), ("zf", 2, 1, 1),
-    ("zf", 2, -1, 1), ("ry", 0, 2), ("zf", 3, 1, "x"), ("xp", 5), ("zf", 3, -1, "x"), ("xp", 6), ("comp", 3),
-    ("ry", 1, 3), ("zf", 3, -1, 0), ("zf", 3, 1, 0), ("comp", 4), ("ry", 0, 1), ("ry", 2, 4), ("zf", 3, -1, 1),
-    ("zf", 3, 1, 1), ("xp", 7), ("comp", 5), ("ry", 1, 2), ("comp", 6), ("ryd", 0), ("ry", 2, 3), ("comp", 7),
-    ("ry", 1, 1), ("ry", 2, 2), ("rxd", 5), ("auxz",), ("ryd", 1), ("ry", 2, 1), ("rxd", 6), ("addz", 2), ("addz", 1),
-    ("bdone", 5), ("auxy",), ("rxd", 7), ("ryd", 2), ("auxx",), ("bdone", 6), ("addz", 4), ("addz", 3), ("last",),
-    ("bdone", 7), ("finish",),
+    ("zs", 1, -1, "x"), ("zs", 1, 1, "x"), ("zs", 1, -1, 1), ("zs", 1, 1, 1), ("pts",), ("stage", 0), ("stage", 1),
+    ("stage", 2), ("keep", 0), ("keep", 1), ("stage", 3), ("keep", 2), ("keep", 3), ("stage", 4), ("stage", 5),
+    ("keep", 4), ("keep", 5), ("stage", 6), ("stage", 7), ("keep", 6), ("keep", 7), ("xp", 2), ("zf", 1, 1, "x"),
+    ("zf", 1, -1, "x"), ("xp", 1), ("zs", 1, -1, 0), ("comp", 0), ("ry", 0, 4), ("zs", 1, 1, 0), ("zf", 1, -1, 1),
+    ("zf", 1, 1, 1), ("xp", 3), ("zf", 2, -1, "x"), ("xp", 4), ("zf", 2, 1, "x"), ("ry", 0, 3), ("zf", 1, -1, 0),
+    ("comp", 2), ("zf", 1, 1, 0), ("comp", 1), ("ry", 1, 4), ("zf", 2, 1, 1), ("zf", 2, -1, 1), ("ry", 0, 2),
+    ("xp", 6), ("zf", 3, -1, "x"), ("zf", 3, 1, "x"), ("xp", 5), ("zf", 2, -1, 0), ("ry", 1, 3), ("comp", 4),
+    ("ry", 0, 1), ("comp", 3), ("ry", 2, 4), ("zf", 3, -1, 1), ("zf", 2, 1, 0), ("xp", 7), ("ry", 1, 2), ("comp", 6),
+    ("ryd", 0), ("ry", 2, 3), ("comp", 5), ("zf", 3, 1, 0), ("ry", 1, 1), ("ry", 2, 2), ("comp", 7), ("rxd", 6),
+    ("ryd", 1), ("ry", 2, 1), ("auxz",), ("addz", 2), ("rxd", 5), ("addz", 1), ("bdone", 6), ("ryd", 2), ("rxd", 7),
+    ("auxy",), ("bdone", 5), ("addz", 3), ("addz", 4), ("last",), ("auxx",), ("bdone", 7), ("finish",),
 )
 
 def kernel(clus, rows, points, coarse, fine, out,
@@ -113,20 +113,21 @@
 
     own_rows = {}
 
-    def send_rows():
+    def fill_rows():
         sub = lax.broadcasted_iota(jnp.int32, (8, 128), 0)
         m = jnp.zeros((8, 128), jnp.int32)
         for s in range(SLOTS):
             m = jnp.where(sub == s, find(s, 1 - core)[1], m)
         rowmsg[...] = m
-        send("rows", rowmsg, rowin, dc=1)
 
     def stage_slot(s):
-        residual(s, 1 - core, stage.at[s])
+        if s not in EARLY:
+            residual(s, 1 - core, stage.at[s])
         send(("res", s), stage.at[s], res.at[s, pl.ds(B, B)], dc=1)
 
     def keep_slot(s):
-        own_rows[s] = residual(s, core, res.at[s, pl.ds(0, B)])
+        if s not in own_rows:
+            own_rows[s] = residual(s, core, res.at[s, pl.ds(0, B)])
 
     def zsend(d, way, name):
         s = 0 if d == 1 else OFF.index(way * (d - 1))
@@ -189,16 +190,17 @@
         lhs = jnp.concatenate([wh, jnp.broadcast_to(live, (16, 2 * B)).astype(BF)], axis=0)
         sub = lax.broadcasted_iota(jnp.int32, (8, 128), 0)
         drift = jnp.zeros((8, 128), F32)
-        for c0 in range(0, D, 128):
-            p = jnp.dot(lhs, r[:, c0:c0 + 128], preferred_element_type=F32)
-            drift = jnp.where(sub == c0 // 128, p[K:K + 8], drift)
+        for c0 in range(0, D, 256):
+            p = jnp.dot(lhs, r[:, c0:c0 + 256], preferred_element_type=F32)
+            for c in (0, 128):
+                drift = jnp.where(sub == (c0 + c) // 128, p[K:K + 8, c:c + 128], drift)
             if s not in FAR:
                 for yy in range(NY):
                     q = jnp.concatenate([p[64 * k + 8 * yy:64 * k + 8 * yy + 8] for k in range(NX)], axis=0)
-                    py[s, yy, :, c0:c0 + 128] = q.astype(BF)
+                    py[s, yy, :, c0:c0 + 256] = q.astype(BF)
             else:
                 for xx in range(NX):
-                    px[s - FAR[0], xx, :, c0:c0 + 128] = p[64 * xx:64 * xx + 64].astype(BF)
+                    px[s - FAR[0], xx, :, c0:c0 + 256] = p[64 * xx:64 * xx + 64].astype(BF)
         seen = jnp.broadcast_to((n + n2).astype(F32), (8, 128))
         more = jnp.where(sub == 0, cnt[:8, :128], jnp.where(sub == 1, cnt[:8, 128:], seen))
         aux[s, 0:8, :] = drift
@@ -228,14 +230,18 @@
         for j in range(1, NY):
             got(("bx", f, j))
             v = v + rbx[f, j - 1].astype(F32)
-        szc[f] = v
+        szc[f] = v.astype(BF)
         send(("zc", f), szc.at[f], rzc.at[f], dz=OFF[f + FAR[0]])
 
-    def rs_y_send(g, dist):
-        for way in (1, -1):
-            sl = GROUPS[g]
-            if dist == 4:
-                sl = sl[:1] if way > 0 else sl[1:]
+    def rs_y_slots(g, dist, way):
+        sl = GROUPS[g]
+        if dist == 4:
+            sl = sl[:1] if way > 0 else sl[1:]
+        return sl
+
+    def rs_y_send(g, dist, ways=(1, -1)):
+        for way in ways:
+            sl = rs_y_slots(g, dist, way)
             if not sl:
                 continue
             to = lax.rem(y + way * dist + NY, NY)
@@ -244,17 +250,18 @@
 
     def rs_y_hop(g, dist):
         for way in (1, -1):
-            if ("ry", g, dist, way) not in made:
-                continue
-            sl = GROUPS[g]
-            if dist == 4:
-                sl = sl[:1] if way > 0 else sl[1:]
-            got(("ry", g, dist, way))
-            to = lax.rem(y + way * (dist - 1) + NY, NY)
-            for s in sl:
-                v = py[s, to].astype(F32) + ry[(way < 0) * 4 + dist - 1, s].astype(F32)
-                py[s, to] = v.astype(BF)
-        rs_y_send(g, dist - 1)
+            if ("ry", g, dist, way) in made:
+                got(("ry", g, dist, way))
+                to = lax.rem(y + way * (dist - 1) + NY, NY)
+                for s in rs_y_slots(g, dist, way):
+                    v = py[s, to].astype(F32) + ry[(way < 0) * 4 + dist - 1, s].astype(F32)
+                    py[s, to] = v.astype(BF)
+            rs_y_send(g, dist - 1, (way,))
+
+    def rs_y_done(g):
+        got_all([("ry", g, 1, 1), ("ry", g, 1, -1)])
+        for s in GROUPS[g]:
+            rs_y_out(s, py[s, y].astype(F32) + ry[0, s].astype(F32) + ry[4, s].astype(F32))
 
     def rs_y_out(s, v):
         if s == 0:
@@ -262,11 +269,6 @@
         else:
             szy[s] = v.astype(BF)
             send(("zy", s), szy.at[s], rzy.at[s], dz=OFF[s])
-
-    def rs_y_done(g):
-        got_all([("ry", g, 1, 1), ("ry", g, 1, -1)])
-        for s in GROUPS[g]:
-            rs_y_out(s, py[s, y].astype(F32) + ry[0, s].astype(F32) + ry[4, s].astype(F32))
 
     def add_z(s):
         got(("zy", s))
@@ -322,18 +324,17 @@
             got(("fy", j))
             v = v + rfy[j - 1]
         got(("zc", 0))
-        far = rzc[0]
+        far = rzc[0].astype(F32)
         for f in range(1, len(FAR)):
             got(("zc", f))
-            far = far + rzc[f]
+            far = far + rzc[f].astype(F32)
         div = made["cnt"] + 1.0
         out[:8, :H] = (v[:, :H] + far[:8]) / div
         out[:8, H:] = (v[:, H:] + far[8:]) / div
 
     def run(kind, *a):
         if kind == "pts":
-            load_pts.wait()
-            send_rows()
+            send("rows", rowmsg, rowin, dc=1)
         elif kind == "zs":
             zsend(*a)
         elif kind == "zf":
@@ -370,12 +371,22 @@
         elif kind == "finish":
             finish()
 
+    fill_rows()
     load_fine.wait()
+    load_pts.wait()
+    for s in EARLY:
+        residual(s, 1 - core, stage.at[s])
+        keep_slot(s)
     pl.semaphore_wait(barrier, len(partners))
     for e in ORDER:
         run(*e)
     for c in started[sent:]:
         c.wait_send()
+
+
+def split(both, new_fine, coarse_shift):
+    new_fine[0] = both[:8]
+    coarse_shift[...] = both[8:9]
 
 
 def per_device(points, block_cluster, block_rows, coarse, fine):
@@ -401,8 +412,8 @@
             pltpu.VMEM((near, 32, D), BF),
             pltpu.VMEM((far, NY, 16, H), BF),
             pltpu.VMEM((far, NY - 1, 16, H), BF),
-            pltpu.VMEM((far, 16, H), F32),
-            pltpu.VMEM((far, 16, H), F32),
+            pltpu.VMEM((far, 16, H), BF),
+            pltpu.VMEM((far, 16, H), BF),
             pltpu.VMEM((NX, 8, D), F32),
             pltpu.VMEM((NX - 1, 8, D), F32),
             pltpu.VMEM((8, 128), jnp.int32),
@@ -420,7 +431,13 @@
         cost_estimate=pl.CostEstimate(flops=8 * 10**9, bytes_accessed=5 * 10**6, transcendentals=10**6),
         name="lloyd",
     )(block_cluster, block_rows, points.reshape(8, B, D), coarse, fine)
-    return both[:8].reshape(1, 8, D), both[8:9]
+    return pl.pallas_call(
+        split,
+        out_shape=(jax.ShapeDtypeStruct((1, 8, D), F32), jax.ShapeDtypeStruct((1, D), F32)),
+        in_specs=[vmem],
+        out_specs=(vmem, vmem),
+        name="split",
+    )(both)
 
 
 def solution(mesh):

time: 84.7 us -> 80.8 us (0.954)
  the two profiles are of different devices: /device:TPU:4 before, /device:TPU:8 now
where the time goes in v3:
time: 80.8 us; the launch traced here: 80.5 us
  Pallas kernels  79.9 us (99%)
    pallas_call x1, Pallas kernels, per_device(): pl.pallas_call(kernel, out_shape=jax.ShapeDtypeStruct((16, D), F32), in_s...  78.4 us

profile of v3, /device:TPU:8, one launch (start us, length us, event | category | flops | bytes accessed | tf_op | source)
XLA Modules:
  0.0 80.5 jit_solution(15415670104417256202)
XLA Ops:
  0.6 78.4 %lloyd.1.both = f32[16,1024]{1,0:T(8,128)} custom-call(s32[8]{0:T(128)} %clus.1, s32[8]{0:T(128)} %rows.1, bf16[8,256,1024]{2,1,0:T(8,128)(2,1)} %bitcast.1, bf16[16,1024]{1,0:T(8,128)(2,1)} %coarse.1, bf16[1,256,1024]{2,1,0:T(8,128)(2,1)} %fine.1), custom_call_target="tpu_custom_call" | custom-call | flops 8000000000 | bytes 5000000 | tf_op jit(solution)/shard_map/lloyd/pallas_call | solution.py:397
  79.1 1.5 %split.1 = (f32[1,8,1024]{2,1,0:T(8,128)}, f32[1,1024]{1,0:T(1,128)}) custom-call(f32[16,1024]{1,0:T(8,128)} %lloyd.1.both), custom_call_target="tpu_custom_call" | custom-call | tf_op jit(solution)/shard_map/split/pallas_call | solution.py:434

commit v4 on v3

--- a/solution.py
+++ b/solution.py
@@ -21,17 +21,17 @@
 MESH = pl.DeviceIdType.MESH
 BF, F32 = jnp.bfloat16, jnp.float32
 ORDER = (
-    ("zs", 1, -1, "x"), ("zs", 1, 1, "x"), ("zs", 1, -1, 1), ("zs", 1, 1, 1), ("pts",), ("stage", 0), ("stage", 1),
-    ("stage", 2), ("keep", 0), ("keep", 1), ("stage", 3), ("keep", 2), ("keep", 3), ("stage", 4), ("stage", 5),
-    ("keep", 4), ("keep", 5), ("stage", 6), ("stage", 7), ("keep", 6), ("keep", 7), ("xp", 2), ("zf", 1, 1, "x"),
-    ("zf", 1, -1, "x"), ("xp", 1), ("zs", 1, -1, 0), ("comp", 0), ("ry", 0, 4), ("zs", 1, 1, 0), ("zf", 1, -1, 1),
-    ("zf", 1, 1, 1), ("xp", 3), ("zf", 2, -1, "x"), ("xp", 4), ("zf", 2, 1, "x"), ("ry", 0, 3), ("zf", 1, -1, 0),
-    ("comp", 2), ("zf", 1, 1, 0), ("comp", 1), ("ry", 1, 4), ("zf", 2, 1, 1), ("zf", 2, -1, 1), ("ry", 0, 2),
-    ("xp", 6), ("zf", 3, -1, "x"), ("zf", 3, 1, "x"), ("xp", 5), ("zf", 2, -1, 0), ("ry", 1, 3), ("comp", 4),
-    ("ry", 0, 1), ("comp", 3), ("ry", 2, 4), ("zf", 3, -1, 1), ("zf", 2, 1, 0), ("xp", 7), ("ry", 1, 2), ("comp", 6),
-    ("ryd", 0), ("ry", 2, 3), ("comp", 5), ("zf", 3, 1, 0), ("ry", 1, 1), ("ry", 2, 2), ("comp", 7), ("rxd", 6),
-    ("ryd", 1), ("ry", 2, 1), ("auxz",), ("addz", 2), ("rxd", 5), ("addz", 1), ("bdone", 6), ("ryd", 2), ("rxd", 7),
-    ("auxy",), ("bdone", 5), ("addz", 3), ("addz", 4), ("last",), ("auxx",), ("bdone", 7), ("finish",),
+    ("zs", 1, -1, "x"), ("zs", 1, 1, "x"), ("zs", 1, -1, 1), ("pts",), ("stage", 0), ("keep", 5), ("stage", 2),
+    ("stage", 5), ("keep", 4), ("zs", 1, 1, 1), ("keep", 0), ("stage", 4), ("keep", 6), ("keep", 7), ("keep", 3),
+    ("stage", 7), ("stage", 1), ("stage", 3), ("stage", 6), ("xp", 2), ("zf", 1, -1, "x"), ("zf", 1, 1, "x"),
+    ("xp", 1), ("zs", 1, -1, 0), ("keep", 2), ("keep", 1), ("comp", 0), ("ry", 0, 4), ("zs", 1, 1, 0),
+    ("zf", 1, -1, 1), ("zf", 1, 1, 1), ("zf", 2, -1, "x"), ("xp", 3), ("xp", 4), ("zf", 2, 1, "x"), ("ry", 0, 3),
+    ("zf", 1, -1, 0), ("comp", 2), ("zf", 1, 1, 0), ("comp", 1), ("zf", 2, -1, 1), ("ry", 1, 4), ("zf", 2, 1, 1),
+    ("ry", 0, 2), ("xp", 6), ("zf", 3, -1, "x"), ("zf", 3, 1, "x"), ("xp", 5), ("zf", 2, -1, 0), ("ry", 1, 3),
+    ("zf", 2, 1, 0), ("comp", 4), ("ry", 0, 1), ("comp", 3), ("zf", 3, -1, 1), ("ry", 2, 4), ("xp", 7), ("ry", 1, 2),
+    ("comp", 6), ("ryd", 0), ("zf", 3, 1, 0), ("comp", 5), ("ry", 2, 3), ("ry", 1, 1), ("comp", 7), ("ry", 2, 2),
+    ("rxd", 6), ("ryd", 1), ("auxz",), ("ry", 2, 1), ("rxd", 5), ("addz", 1), ("addz", 2), ("bdone", 6), ("auxy",),
+    ("rxd", 7), ("ryd", 2), ("auxx",), ("bdone", 5), ("addz", 3), ("addz", 4), ("last",), ("bdone", 7), ("finish",),
 )
 
 def kernel(clus, rows, points, coarse, fine, out,

time: 80.8 us -> 79.5 us (0.984)
  Pallas kernels: 79.9 us -> 78.6 us
    pallas_call x1, Pallas kernels: 78.4 us -> 77.1 us  [per_device(): pl.pallas_call(kernel, out_shape=jax.ShapeDtypeStruct((16, D), F32), in_s...]
where the time goes in v4:
time: 79.5 us; the launch traced here: 79.2 us
  Pallas kernels  78.6 us (99%)
    pallas_call x1, Pallas kernels, per_device(): pl.pallas_call(kernel, out_shape=jax.ShapeDtypeStruct((16, D), F32), in_s...  77.1 us

profile of v4, /device:TPU:8, one launch (start us, length us, event | category | flops | bytes accessed | tf_op | source)
XLA Modules:
  0.0 79.2 jit_solution(16364344159690160665)
XLA Ops:
  0.6 77.1 %lloyd.1.both = f32[16,1024]{1,0:T(8,128)} custom-call(s32[8]{0:T(128)} %clus.1, s32[8]{0:T(128)} %rows.1, bf16[8,256,1024]{2,1,0:T(8,128)(2,1)} %bitcast.1, bf16[16,1024]{1,0:T(8,128)(2,1)} %coarse.1, bf16[1,256,1024]{2,1,0:T(8,128)(2,1)} %fine.1), custom_call_target="tpu_custom_call" | custom-call | flops 8000000000 | bytes 5000000 | tf_op jit(solution)/shard_map/lloyd/pallas_call | solution.py:397
  77.8 1.5 %split.1 = (f32[1,8,1024]{2,1,0:T(8,128)}, f32[1,1024]{1,0:T(1,128)}) custom-call(f32[16,1024]{1,0:T(8,128)} %lloyd.1.both), custom_call_target="tpu_custom_call" | custom-call | tf_op jit(solution)/shard_map/split/pallas_call | solution.py:434
